TPU v7x, 32 devices: a whole 2x2x4 slice. The times are simulated.
32 devices in a mesh: parts: 2 (over x), ctx: 16 (over z, y, core).
Axes of the slice: x: 2, y: 2, z: 4, core: 2. Of those that a mesh axis runs over, the one named last changes fastest.
Arguments:
- query_rows: bfloat16 [2, 4096, 1536], P(None, ('parts', 'ctx')), parts along dimension 1, may hold values from -6 to 6
- key_rows: bfloat16 [2, 4096, 1536], P(None, ('parts', 'ctx')), parts along dimension 1, may hold values from -4 to 4
- value_rows: bfloat16 [2, 4096, 1536], P(None, ('parts', 'ctx')), parts along dimension 1, may hold values from -12 to 12
- step_rates: float32 [2, 4096, 4], P(None, ('parts', 'ctx')), parts along dimension 1, may hold values from 0.01 to 1
- gate_weight: float32 [3072, 384], P(('parts', 'ctx')), parts along dimension 0, may hold values from -0.3125 to 0.3125
- up_weight: float32 [3072, 384], P(('parts', 'ctx')), parts along dimension 0, may hold values from -0.3125 to 0.3125
- down_weight: float32 [3072, 384], P(('parts', 'ctx')), parts along dimension 0, may hold values from -0.3125 to 0.3125
Outputs:
- attended: bfloat16 [2, 4096, 1536], P(None, ('parts', 'ctx')), parts along dimension 1
- gate_next: float32 [3072, 384], P(('parts', 'ctx')), parts along dimension 0
- up_next: float32 [3072, 384], P(('parts', 'ctx')), parts along dimension 0
- down_next: float32 [3072, 384], P(('parts', 'ctx')), parts along dimension 0
There are 2 independent parts, one for each index of `parts`. A program takes and returns all parts, laid end to end along the dimension named above; each array names one. Nothing has to cross between parts.
All inputs are finite; a program needn't handle non-finite values.
Results may differ from a plain program's by a relative error of at most 0.0081.
Values may be sent and summed in bfloat16 or wider, within the bound.
A program may use at most 64 MiB of HBM per device.

v0:
```python
import math

import jax
import jax.numpy as jnp
from jax import lax
from jax.sharding import PartitionSpec as P


def from_partner(value, axis, apart):
    mask = 2**apart
    pairs = [(source, source ^ mask) for source in range(lax.axis_size(axis))]
    return lax.ppermute(value, axis, pairs)


def silu_parts(values):
    sig = jax.nn.sigmoid(values)
    return (values * sig, sig * (1.0 + values * (1.0 - sig)))


def span_pass(queries, keys_here, scaled_rows, gate_low, up_low, down_low, heads):
    count = queries.shape[0]
    width = gate_low.shape[1]
    hidden = gate_low.shape[0] // heads
    gate_three = gate_low.reshape(heads, hidden, width)
    up_three = up_low.reshape(heads, hidden, width)
    down_three = down_low.reshape(heads, width, hidden)
    key_three = keys_here.reshape(count, heads, width)
    first = jnp.einsum("thd,hfd->thf", key_three, gate_three, preferred_element_type=jnp.float32)
    second = jnp.einsum("thd,hfd->thf", key_three, up_three, preferred_element_type=jnp.float32)
    silu_first, slope = silu_parts(first)
    acts = (silu_first * second).astype(jnp.bfloat16)
    scaled = scaled_rows.reshape(count, heads, width)
    back = jnp.einsum("thd,hdf->thf", scaled, down_three, preferred_element_type=jnp.float32)
    d_gate = (back * second * slope).astype(jnp.bfloat16)
    d_up = (back * silu_first).astype(jnp.bfloat16)
    grad_gate = jnp.einsum(
        "thf,thd->hfd", d_gate, key_three, preferred_element_type=jnp.float32
    ).reshape(heads * hidden, width)
    grad_up = jnp.einsum(
        "thf,thd->hfd", d_up, key_three, preferred_element_type=jnp.float32
    ).reshape(heads * hidden, width)
    grad_down = jnp.einsum(
        "thd,thf->hdf", scaled, acts, preferred_element_type=jnp.float32
    ).reshape(heads * width, hidden)
    query_three = queries.reshape(count, heads, width)
    query_gate = jnp.einsum(
        "thd,hfd->thf", query_three, gate_three, preferred_element_type=jnp.float32
    )
    query_up = jnp.einsum("thd,hfd->thf", query_three, up_three, preferred_element_type=jnp.float32)
    query_acts = (jax.nn.silu(query_gate) * query_up).astype(jnp.bfloat16)
    output = jnp.einsum("thf,hdf->thd", query_acts, down_three, preferred_element_type=jnp.float32)
    return (
        output.reshape(count, heads * width).astype(jnp.bfloat16),
        (grad_gate, grad_up, grad_down),
    )


def head_member(row_count, offset, per_head, heads):
    row_ids = offset + jnp.arange(row_count, dtype=jnp.int32)
    head_ids = jnp.arange(heads, dtype=jnp.int32)
    return (row_ids[:, None] // per_head == head_ids[None, :]).astype(jnp.float32)


def head_partial(gradient, member):
    return jnp.sum(member * jnp.sum(gradient * gradient, axis=1)[:, None], axis=0)


def refresh_rows(matrix, gradient, member, head_total, per_head):
    columns = matrix.shape[1]
    block_mean = head_total / (per_head * columns)
    factor = lax.rsqrt(block_mean + 1e-06) / math.sqrt(columns)
    row_factor = jnp.sum(member * factor[None, :], axis=1)
    stepped = matrix + gradient * row_factor[:, None]
    row_mean = jnp.mean(stepped * stepped, axis=1, keepdims=True)
    return stepped * lax.rsqrt(row_mean + 1e-06) / math.sqrt(columns)


def update_shards(masters, shares, heads):
    row_count = masters[0].shape[0]
    total_rows = row_count * lax.axis_size("ctx")
    per_head = total_rows // heads
    offset = lax.axis_index("ctx") * row_count
    member = head_member(row_count, offset, per_head, heads)
    partials = [head_partial(shares[i], member) for i in range(3)]
    totals = lax.psum((partials[0], partials[1], partials[2]), "ctx")
    return tuple(
        (refresh_rows(masters[i], shares[i], member, totals[i], per_head) for i in range(3))
    )


def scale_values(value_rows, step_rates):
    span_count, count, total_width = value_rows.shape
    heads = step_rates.shape[2]
    spread = value_rows.reshape(span_count, count, heads, total_width // heads).astype(jnp.float32)
    return (
        (step_rates[:, :, :, None] * spread)
        .astype(jnp.bfloat16)
        .reshape(span_count, count, total_width)
    )


def to_heads(array, groups, heads):
    span_count, count, total_width = array.shape
    slab = count // groups
    width = total_width // heads
    spread = array.reshape(span_count, groups, slab, heads, width).transpose(3, 1, 0, 2, 4)
    return spread.reshape(heads * groups, span_count, slab, width)


def from_heads(array, groups, heads):
    devices, span_count, slab, width = array.shape
    spread = array.reshape(heads, groups, span_count, slab, width).transpose(2, 1, 3, 0, 4)
    return spread.reshape(span_count, groups * slab, heads * width)


def per_device(query_rows, key_rows, value_rows, step_rates, gate_weight, up_weight, down_weight):
    heads = step_rates.shape[2]
    span_count = query_rows.shape[0]
    scaled_all = scale_values(value_rows, step_rates)
    results = []
    groups = lax.axis_size("ctx") // heads
    bits = groups.bit_length() - 1
    position = lax.axis_index("ctx")
    moved = (
        lax.all_to_all(
            to_heads(query_rows, groups, heads), "ctx", split_axis=0, concat_axis=0, tiled=True
        ),
        lax.all_to_all(
            to_heads(key_rows, groups, heads), "ctx", split_axis=0, concat_axis=0, tiled=True
        ),
        lax.all_to_all(
            to_heads(scaled_all, groups, heads), "ctx", split_axis=0, concat_axis=0, tiled=True
        ),
    )
    width = moved[0].shape[3]
    masters = (gate_weight, up_weight, down_weight)
    for span_index in range(span_count):
        blocks = tuple((matrix.astype(jnp.bfloat16) for matrix in masters))
        for level in range(bits):
            other = from_partner((blocks[0], blocks[1], blocks[2]), "ctx", level)
            upper_side = position >> level & 1 == 1
            blocks = tuple(
                (
                    jnp.where(
                        upper_side,
                        jnp.concatenate([other[i], blocks[i]], axis=0),
                        jnp.concatenate([blocks[i], other[i]], axis=0),
                    )
                    for i in range(3)
                )
            )
        queries = moved[0][:, span_index].reshape(-1, width)
        keys_here = moved[1][:, span_index].reshape(-1, width)
        scaled_rows = moved[2][:, span_index].reshape(-1, width)
        output, grads = span_pass(
            queries, keys_here, scaled_rows, blocks[0], blocks[1], blocks[2], 1
        )
        results.append(output.reshape(moved[0].shape[0], moved[0].shape[2], width))
        for level in reversed(range(bits)):
            upper_side = position >> level & 1 == 1
            halves = [grad.shape[0] // 2 for grad in grads]
            kept = tuple(
                (
                    jnp.where(upper_side, grads[i][halves[i] :], grads[i][: halves[i]])
                    for i in range(3)
                )
            )
            sent = tuple(
                (
                    jnp.where(upper_side, grads[i][: halves[i]], grads[i][halves[i] :])
                    for i in range(3)
                )
            )
            other = from_partner((sent[0], sent[1], sent[2]), "ctx", level)
            grads = tuple((kept[i] + other[i] for i in range(3)))
        masters = update_shards(masters, grads, heads)
    stacked = jnp.stack(results, axis=1)
    returned = lax.all_to_all(stacked, "ctx", split_axis=0, concat_axis=0, tiled=True)
    return (from_heads(returned, groups, heads), masters[0], masters[1], masters[2])


def solution(mesh):
    placed = (
        P(None, ("parts", "ctx"), None),
        P(None, ("parts", "ctx"), None),
        P(None, ("parts", "ctx"), None),
        P(None, ("parts", "ctx"), None),
        P(("parts", "ctx"), None),
        P(("parts", "ctx"), None),
        P(("parts", "ctx"), None),
    )
    return jax.shard_map(
        per_device,
        mesh=mesh,
        in_specs=placed,
        out_specs=(
            P(None, ("parts", "ctx"), None),
            P(("parts", "ctx"), None),
            P(("parts", "ctx"), None),
            P(("parts", "ctx"), None),
        ),
        check_vma=False,
    )
```

profile of v0, /device:TPU:0, one launch (start us, length us, event | category | flops | bytes accessed | tf_op | source)
XLA Modules:
  0.0 230.3 jit_solution(16068693881314801204)
XLA Ops:
  0.6 1.8 reshape.396
  3.4 7.4 %all-to-all-start.2 = ((bf16[16,2,32,384]{3,2,1,0:T(8,128)(2,1)}), bf16[16,2,32,384]{3,2,1,0:T(8,128)(2,1)S(1)}, u32[]{:S(2)}, u32[]{:S(2)}) async-start(bf16[16,2,32,384]{3,2,1,0:T(8,128)(2,1)} %bitcast.17), calls=%async_computation.2 | async-start | bytes 1572864 | tf_op jit(solution)/shard_map/all_to_all | solution.py:128
  12.9 16.6 %all-to-all-done.2 = bf16[16,2,32,384]{3,2,1,0:T(8,128)(2,1)S(1)} async-done(((bf16[16,2,32,384]{3,2,1,0:T(8,128)(2,1)}), bf16[16,2,32,384]{3,2,1,0:T(8,128)(2,1)S(1)}, u32[]{:S(2)}, u32[]{:S(2)}) %all-to-all-start.2) | async-done | bytes 786464 | tf_op jit(solution)/shard_map/all_to_all | solution.py:128
  29.5 5.5 %all-to-all-start.1 = ((bf16[16,2,32,384]{3,2,1,0:T(8,128)(2,1)}), bf16[16,2,32,384]{3,2,1,0:T(8,128)(2,1)S(1)}, u32[]{:S(2)}, u32[]{:S(2)}) async-start(bf16[16,2,32,384]{3,2,1,0:T(8,128)(2,1)} %bitcast.14), calls=%async_computation.1 | async-start | bytes 1572864 | tf_op jit(solution)/shard_map/all_to_all | solution.py:131
  38.0 1.7 collective-permute-start.3
  45.4 8.4 %all-to-all-done.1 = bf16[16,2,32,384]{3,2,1,0:T(8,128)(2,1)S(1)} async-done(((bf16[16,2,32,384]{3,2,1,0:T(8,128)(2,1)}), bf16[16,2,32,384]{3,2,1,0:T(8,128)(2,1)S(1)}, u32[]{:S(2)}, u32[]{:S(2)}) %all-to-all-start.1) | async-done | bytes 786464 | tf_op jit(solution)/shard_map/all_to_all | solution.py:131
  53.8 5.5 %all-to-all-start = ((bf16[16,2,32,384]{3,2,1,0:T(8,128)(2,1)}), bf16[16,2,32,384]{3,2,1,0:T(8,128)(2,1)S(1)}, u32[]{:S(2)}, u32[]{:S(2)}) async-start(bf16[16,2,32,384]{3,2,1,0:T(8,128)(2,1)} %bitcast.1), calls=%async_computation | async-start | bytes 1572864 | tf_op jit(solution)/shard_map/all_to_all | solution.py:125
  64.1 1.9 collective-permute-start.6
  68.5 9.5 %all-to-all-done = bf16[16,2,32,384]{3,2,1,0:T(8,128)(2,1)S(1)} async-done(((bf16[16,2,32,384]{3,2,1,0:T(8,128)(2,1)}), bf16[16,2,32,384]{3,2,1,0:T(8,128)(2,1)S(1)}, u32[]{:S(2)}, u32[]{:S(2)}) %all-to-all-start) | async-done | bytes 786464 | tf_op jit(solution)/shard_map/all_to_all | solution.py:125
  78.9 2.3 convolution_bitcast_fusion.9
  81.1 2.3 fusion.4
  87.0 6.6 %collective-permute-done.10 = f32[192,384]{1,0:T(8,128)S(1)} collective-permute-done((f32[192,384]{1,0:T(8,128)S(1)}, f32[192,384]{1,0:T(8,128)S(1)}, u32[]{:S(2)}, u32[]{:S(2)}) %collective-permute-start.10) | collective-permute-done | bytes 294944 | tf_op jit(solution)/shard_map/ppermute | solution.py:12
  93.7 5.5 %collective-permute-done.14 = f32[192,384]{1,0:T(8,128)S(1)} collective-permute-done((f32[192,384]{1,0:T(8,128)S(1)}, f32[192,384]{1,0:T(8,128)S(1)}, u32[]{:S(2)}, u32[]{:S(2)}) %collective-permute-start.14) | collective-permute-done | bytes 294944 | tf_op jit(solution)/shard_map/ppermute | solution.py:12
  101.0 33.6 %all-reduce.1 = (f32[4]{0:T(128)S(1)}, f32[4]{0:T(128)S(1)}, f32[4]{0:T(128)S(1)}) all-reduce(f32[4]{0:T(128)S(1)} %get-tuple-element.13, f32[4]{0:T(128)S(1)} %get-tuple-element.14, f32[4]{0:T(128)S(1)} %get-tuple-element.15), channel_id=1, replica_groups=mesh['parts'=2,'ctx'=16] {'ctx'}, use_global_device_ids=true, to_apply=%region_2.3 | all-reduce | flops 12 | bytes 96 | tf_op jit(solution)/shard_map/psum | solution.py:85
  139.8 4.0 %collective-permute-done.13 = bf16[192,384]{1,0:T(8,128)(2,1)S(1)} collective-permute-done((bf16[192,384]{1,0:T(8,128)(2,1)S(1)}, bf16[192,384]{1,0:T(8,128)(2,1)S(1)}, u32[]{:S(2)}, u32[]{:S(2)}) %collective-permute-start.13) | collective-permute-done | bytes 147488 | tf_op jit(solution)/shard_map/ppermute | solution.py:12
  144.2 2.8 %collective-permute-done.17 = bf16[192,384]{1,0:T(8,128)(2,1)S(1)} collective-permute-done((bf16[192,384]{1,0:T(8,128)(2,1)S(1)}, bf16[192,384]{1,0:T(8,128)(2,1)S(1)}, u32[]{:S(2)}, u32[]{:S(2)}) %collective-permute-start.17) | collective-permute-done | bytes 147488 | tf_op jit(solution)/shard_map/ppermute | solution.py:12
  153.5 2.3 fusion.5
  157.1 3.6 %all-to-all-start.3 = ((bf16[16,2,32,384]{3,2,1,0:T(8,128)(2,1)}), bf16[16,2,32,384]{3,2,1,0:T(8,128)(2,1)S(1)}, u32[]{:S(2)}, u32[]{:S(2)}) async-start(bf16[16,2,32,384]{3,2,1,0:T(8,128)(2,1)} %copy.38), calls=%async_computation.3 | async-start | bytes 1572864 | tf_op jit(solution)/shard_map/all_to_all | solution.py:178
  160.7 1.9 collective-permute-start.22
  163.0 1.9 collective-permute-start.20
  164.8 12.1 %collective-permute-done.22 = f32[192,384]{1,0:T(8,128)S(1)} collective-permute-done((f32[192,384]{1,0:T(8,128)S(1)}, f32[192,384]{1,0:T(8,128)S(1)}, u32[]{:S(2)}, u32[]{:S(2)}) %collective-permute-start.22) | collective-permute-done | bytes 294944 | tf_op jit(solution)/shard_map/ppermute | solution.py:12
  177.1 8.2 %collective-permute-done.18 = f32[192,384]{1,0:T(8,128)S(1)} collective-permute-done((f32[192,384]{1,0:T(8,128)S(1)}, f32[192,384]{1,0:T(8,128)S(1)}, u32[]{:S(2)}, u32[]{:S(2)}) %collective-permute-start.18) | collective-permute-done | bytes 294944 | tf_op jit(solution)/shard_map/ppermute | solution.py:12
  185.4 5.7 %collective-permute-done.20 = f32[192,384]{1,0:T(8,128)S(1)} collective-permute-done((f32[192,384]{1,0:T(8,128)S(1)}, f32[192,384]{1,0:T(8,128)S(1)}, u32[]{:S(2)}, u32[]{:S(2)}) %collective-permute-start.20) | collective-permute-done | bytes 294944 | tf_op jit(solution)/shard_map/ppermute | solution.py:12
  192.9 32.6 %all-reduce = (f32[4]{0:T(128)S(1)}, f32[4]{0:T(128)S(1)}, f32[4]{0:T(128)S(1)}) all-reduce(f32[4]{0:T(128)S(1)} %get-tuple-element.7, f32[4]{0:T(128)S(1)} %get-tuple-element.8, f32[4]{0:T(128)S(1)} %get-tuple-element.9), channel_id=1, replica_groups=mesh['parts'=2,'ctx'=16] {'ctx'}, use_global_device_ids=true, to_apply=%region_27.28 | all-reduce | flops 12 | bytes 96 | tf_op jit(solution)/shard_map/psum | solution.py:85
  (162 shorter events, 45.6 us)
Async XLA Ops:
  3.4 26.1 %all-to-all-start.2 = ((bf16[16,2,32,384]{3,2,1,0:T(8,128)(2,1)}), bf16[16,2,32,384]{3,2,1,0:T(8,128)(2,1)S(1)}, u32[]{:S(2)}, u32[]{:S(2)}) async-start(bf16[16,2,32,384]{3,2,1,0:T(8,128)(2,1)} %bitcast.17), calls=%async_computation.2 | async-start | bytes 1572864 | tf_op jit(solution)/shard_map/all_to_all | solution.py:128
  29.5 24.2 %all-to-all-start.1 = ((bf16[16,2,32,384]{3,2,1,0:T(8,128)(2,1)}), bf16[16,2,32,384]{3,2,1,0:T(8,128)(2,1)S(1)}, u32[]{:S(2)}, u32[]{:S(2)}) async-start(bf16[16,2,32,384]{3,2,1,0:T(8,128)(2,1)} %bitcast.14), calls=%async_computation.1 | async-start | bytes 1572864 | tf_op jit(solution)/shard_map/all_to_all | solution.py:131
  35.0 6.2 %collective-permute-start = (bf16[96,384]{1,0:T(8,128)(2,1)S(1)}, bf16[96,384]{1,0:T(8,128)(2,1)}, u32[]{:S(2)}, u32[]{:S(2)}) collective-permute-start(bf16[96,384]{1,0:T(8,128)(2,1)S(1)} %convert_element_type.93), channel_id=1, source_target_pairs={{0,1},{1,0},{2,3},{3,2},{4,5},{5,4},{6,7},{7,6},{8,9},{9,8},{10,11... | collective-permute-start | bytes 221192 | tf_op jit(solution)/shard_map/ppermute | solution.py:12
  36.2 3.6 %collective-permute-start.4 = (bf16[96,384]{1,0:T(8,128)(2,1)}, bf16[96,384]{1,0:T(8,128)(2,1)}, u32[]{:S(2)}, u32[]{:S(2)}) collective-permute-start(bf16[96,384]{1,0:T(8,128)(2,1)} %convert_element_type.95), channel_id=1, source_target_pairs={{0,1},{1,0},{2,3},{3,2},{4,5},{5,4},{6,7},{7,6},{8,9},{9,8},{10,11... | collective-permute-start | bytes 221192 | tf_op jit(solution)/shard_map/ppermute | solution.py:12
  36.3 1.7 collective-permute-start.2
  38.0 22.1 %collective-permute-start.3 = (bf16[192,384]{1,0:T(8,128)(2,1)S(1)}, bf16[192,384]{1,0:T(8,128)(2,1)}, u32[]{:S(2)}, u32[]{:S(2)}) collective-permute-start(bf16[192,384]{1,0:T(8,128)(2,1)S(1)} %maximum_select_fusion.7), channel_id=1, source_target_pairs={{0,2},{1,3},{2,0},{3,1},{4,6},{5,7},{6,4},{7,5},{8,10},{9,11},{10,... | collective-permute-start | bytes 442376 | tf_op jit(solution)/shard_map/ppermute | solution.py:12
  40.8 20.7 %collective-permute-start.5 = (bf16[192,384]{1,0:T(8,128)(2,1)S(1)}, bf16[192,384]{1,0:T(8,128)(2,1)}, u32[]{:S(2)}, u32[]{:S(2)}) collective-permute-start(bf16[192,384]{1,0:T(8,128)(2,1)S(1)} %maximum_select_fusion.8), channel_id=1, source_target_pairs={{0,2},{1,3},{2,0},{3,1},{4,6},{5,7},{6,4},{7,5},{8,10},{9,11},{10,... | collective-permute-start | bytes 442376 | tf_op jit(solution)/shard_map/ppermute | solution.py:12
  42.9 23.2 %collective-permute-start.1 = (bf16[192,384]{1,0:T(8,128)(2,1)}, bf16[192,384]{1,0:T(8,128)(2,1)}, u32[]{:S(2)}, u32[]{:S(2)}) collective-permute-start(bf16[192,384]{1,0:T(8,128)(2,1)} %maximum_select_fusion.6), channel_id=1, source_target_pairs={{0,2},{1,3},{2,0},{3,1},{4,6},{5,7},{6,4},{7,5},{8,10},{9,11},{10,... | collective-permute-start | bytes 442376 | tf_op jit(solution)/shard_map/ppermute | solution.py:12
  53.8 24.2 %all-to-all-start = ((bf16[16,2,32,384]{3,2,1,0:T(8,128)(2,1)}), bf16[16,2,32,384]{3,2,1,0:T(8,128)(2,1)S(1)}, u32[]{:S(2)}, u32[]{:S(2)}) async-start(bf16[16,2,32,384]{3,2,1,0:T(8,128)(2,1)} %bitcast.1), calls=%async_computation | async-start | bytes 1572864 | tf_op jit(solution)/shard_map/all_to_all | solution.py:125
  64.1 21.7 %collective-permute-start.6 = (f32[192,384]{1,0:T(8,128)}, f32[192,384]{1,0:T(8,128)}, u32[]{:S(2)}, u32[]{:S(2)}) collective-permute-start(f32[192,384]{1,0:T(8,128)} %slice_select_fusion.5), channel_id=1, source_target_pairs={{0,2},{1,3},{2,0},{3,1},{4,6},{5,7},{6,4},{7,5},{8,10},{9,11},{10,... | collective-permute-start | bytes 884744 | tf_op jit(solution)/shard_map/ppermute | solution.py:12
  83.6 9.9 %collective-permute-start.10 = (f32[192,384]{1,0:T(8,128)S(1)}, f32[192,384]{1,0:T(8,128)S(1)}, u32[]{:S(2)}, u32[]{:S(2)}) collective-permute-start(f32[192,384]{1,0:T(8,128)S(1)} %slice_select_fusion.4), channel_id=1, source_target_pairs={{0,2},{1,3},{2,0},{3,1},{4,6},{5,7},{6,4},{7,5},{8,10},{9,11},{10,... | collective-permute-start | bytes 884744 | tf_op jit(solution)/shard_map/ppermute | solution.py:12
  84.9 14.3 %collective-permute-start.14 = (f32[192,384]{1,0:T(8,128)S(1)}, f32[192,384]{1,0:T(8,128)S(1)}, u32[]{:S(2)}, u32[]{:S(2)}) collective-permute-start(f32[192,384]{1,0:T(8,128)S(1)} %slice_select_fusion.3), channel_id=1, source_target_pairs={{0,2},{1,3},{2,0},{3,1},{4,6},{5,7},{6,4},{7,5},{8,10},{9,11},{10,... | collective-permute-start | bytes 884744 | tf_op jit(solution)/shard_map/ppermute | solution.py:12
  86.9 12.5 %collective-permute-start.7 = (f32[96,384]{1,0:T(8,128)S(1)}, f32[96,384]{1,0:T(8,128)S(1)}, u32[]{:S(2)}, u32[]{:S(2)}) collective-permute-start(f32[96,384]{1,0:T(8,128)S(1)} %slice_select_fusion.11), channel_id=1, source_target_pairs={{0,1},{1,0},{2,3},{3,2},{4,5},{5,4},{6,7},{7,6},{8,9},{9,8},{10,11... | collective-permute-start | bytes 442376 | tf_op jit(solution)/shard_map/ppermute | solution.py:12
  93.6 5.9 %collective-permute-start.11 = (f32[96,384]{1,0:T(8,128)S(1)}, f32[96,384]{1,0:T(8,128)S(1)}, u32[]{:S(2)}, u32[]{:S(2)}) collective-permute-start(f32[96,384]{1,0:T(8,128)S(1)} %slice_select_fusion.10), channel_id=1, source_target_pairs={{0,1},{1,0},{2,3},{3,2},{4,5},{5,4},{6,7},{7,6},{8,9},{9,8},{10,11... | collective-permute-start | bytes 442376 | tf_op jit(solution)/shard_map/ppermute | solution.py:12
  135.4 3.9 %collective-permute-start.8 = (bf16[96,384]{1,0:T(8,128)(2,1)S(1)}, bf16[96,384]{1,0:T(8,128)(2,1)S(1)}, u32[]{:S(2)}, u32[]{:S(2)}) collective-permute-start(bf16[96,384]{1,0:T(8,128)(2,1)S(1)} %fusion.33), channel_id=1, source_target_pairs={{0,1},{1,0},{2,3},{3,2},{4,5},{5,4},{6,7},{7,6},{8,9},{9,8},{10,11... | collective-permute-start | bytes 221192 | tf_op jit(solution)/shard_map/ppermute | solution.py:12
  137.1 6.7 %collective-permute-start.13 = (bf16[192,384]{1,0:T(8,128)(2,1)S(1)}, bf16[192,384]{1,0:T(8,128)(2,1)S(1)}, u32[]{:S(2)}, u32[]{:S(2)}) collective-permute-start(bf16[192,384]{1,0:T(8,128)(2,1)S(1)} %maximum_select_fusion.10), channel_id=1, source_target_pairs={{0,2},{1,3},{2,0},{3,1},{4,6},{5,7},{6,4},{7,5},{8,10},{9,11},{10,... | collective-permute-start | bytes 442376 | tf_op jit(solution)/shard_map/ppermute | solution.py:12
  137.6 9.4 %collective-permute-start.17 = (bf16[192,384]{1,0:T(8,128)(2,1)S(1)}, bf16[192,384]{1,0:T(8,128)(2,1)S(1)}, u32[]{:S(2)}, u32[]{:S(2)}) collective-permute-start(bf16[192,384]{1,0:T(8,128)(2,1)S(1)} %maximum_select_fusion.11), channel_id=1, source_target_pairs={{0,2},{1,3},{2,0},{3,1},{4,6},{5,7},{6,4},{7,5},{8,10},{9,11},{10,... | collective-permute-start | bytes 442376 | tf_op jit(solution)/shard_map/ppermute | solution.py:12
  139.3 10.2 %collective-permute-start.9 = (bf16[192,384]{1,0:T(8,128)(2,1)S(1)}, bf16[192,384]{1,0:T(8,128)(2,1)S(1)}, u32[]{:S(2)}, u32[]{:S(2)}) collective-permute-start(bf16[192,384]{1,0:T(8,128)(2,1)S(1)} %maximum_select_fusion.9), channel_id=1, source_target_pairs={{0,2},{1,3},{2,0},{3,1},{4,6},{5,7},{6,4},{7,5},{8,10},{9,11},{10,... | collective-permute-start | bytes 442376 | tf_op jit(solution)/shard_map/ppermute | solution.py:12
  157.1 71.4 %all-to-all-start.3 = ((bf16[16,2,32,384]{3,2,1,0:T(8,128)(2,1)}), bf16[16,2,32,384]{3,2,1,0:T(8,128)(2,1)S(1)}, u32[]{:S(2)}, u32[]{:S(2)}) async-start(bf16[16,2,32,384]{3,2,1,0:T(8,128)(2,1)} %copy.38), calls=%async_computation.3 | async-start | bytes 1572864 | tf_op jit(solution)/shard_map/all_to_all | solution.py:178
  160.7 16.2 %collective-permute-start.22 = (f32[192,384]{1,0:T(8,128)S(1)}, f32[192,384]{1,0:T(8,128)S(1)}, u32[]{:S(2)}, u32[]{:S(2)}) collective-permute-start(f32[192,384]{1,0:T(8,128)S(1)} %slice_select_fusion), channel_id=1, source_target_pairs={{0,2},{1,3},{2,0},{3,1},{4,6},{5,7},{6,4},{7,5},{8,10},{9,11},{10,... | collective-permute-start | bytes 884744 | tf_op jit(solution)/shard_map/ppermute | solution.py:12
  162.6 22.6 %collective-permute-start.18 = (f32[192,384]{1,0:T(8,128)S(1)}, f32[192,384]{1,0:T(8,128)S(1)}, u32[]{:S(2)}, u32[]{:S(2)}) collective-permute-start(f32[192,384]{1,0:T(8,128)S(1)} %slice_select_fusion.2), channel_id=1, source_target_pairs={{0,2},{1,3},{2,0},{3,1},{4,6},{5,7},{6,4},{7,5},{8,10},{9,11},{10,... | collective-permute-start | bytes 884744 | tf_op jit(solution)/shard_map/ppermute | solution.py:12
  163.0 28.1 %collective-permute-start.20 = (f32[192,384]{1,0:T(8,128)S(1)}, f32[192,384]{1,0:T(8,128)S(1)}, u32[]{:S(2)}, u32[]{:S(2)}) collective-permute-start(f32[192,384]{1,0:T(8,128)S(1)} %slice_select_fusion.1), channel_id=1, source_target_pairs={{0,2},{1,3},{2,0},{3,1},{4,6},{5,7},{6,4},{7,5},{8,10},{9,11},{10,... | collective-permute-start | bytes 884744 | tf_op jit(solution)/shard_map/ppermute | solution.py:12
  177.0 14.3 %collective-permute-start.23 = (f32[96,384]{1,0:T(8,128)S(1)}, f32[96,384]{1,0:T(8,128)S(1)}, u32[]{:S(2)}, u32[]{:S(2)}) collective-permute-start(f32[96,384]{1,0:T(8,128)S(1)} %slice_select_fusion.6), channel_id=1, source_target_pairs={{0,1},{1,0},{2,3},{3,2},{4,5},{5,4},{6,7},{7,6},{8,9},{9,8},{10,11... | collective-permute-start | bytes 442376 | tf_op jit(solution)/shard_map/ppermute | solution.py:12
  185.3 6.1 %collective-permute-start.19 = (f32[96,384]{1,0:T(8,128)S(1)}, f32[96,384]{1,0:T(8,128)S(1)}, u32[]{:S(2)}, u32[]{:S(2)}) collective-permute-start(f32[96,384]{1,0:T(8,128)S(1)} %slice_select_fusion.8), channel_id=1, source_target_pairs={{0,1},{1,0},{2,3},{3,2},{4,5},{5,4},{6,7},{7,6},{8,9},{9,8},{10,11... | collective-permute-start | bytes 442376 | tf_op jit(solution)/shard_map/ppermute | solution.py:12
  (21 other events, 284.6 us)
where the time goes:
time: 231 us; the launch traced here: 230 us
  waiting for transfers between devices  84.4 us (37%)
  blocking collectives  66.1 us (29%)
  starting transfers between devices  38.4 us (17%)
  matrix products  16.1 us (7%)
  local copies, waits for them, and re-layouts  12.8 us (6%)
  other arithmetic  11.1 us (5%)
    psum x2, blocking collectives, update_shards(): totals = lax.psum((partials[0], partials[1], partials[2]), 'ctx')  66.1 us
    ppermute x24, waiting for transfers between devices, from_partner(): return lax.ppermute(value, axis, pairs)  49.9 us
    all_to_all x1, waiting for transfers between devices, per_device(): lax.all_to_all(to_heads(key_rows, groups, heads), 'ctx', split_axis=0, co...  16.6 us
    ppermute x24, starting transfers between devices, from_partner(): return lax.ppermute(value, axis, pairs)  16.4 us
    all_to_all x1, waiting for transfers between devices, per_device(): lax.all_to_all(to_heads(query_rows, groups, heads), 'ctx', split_axis=0,...  9.54 us
    all_to_all x1, waiting for transfers between devices, per_device(): lax.all_to_all(to_heads(scaled_all, groups, heads), 'ctx', split_axis=0,...  8.38 us
    all_to_all x1, starting transfers between devices, per_device(): lax.all_to_all(to_heads(key_rows, groups, heads), 'ctx', split_axis=0, co...  7.39 us
    all_to_all x1, starting transfers between devices, per_device(): lax.all_to_all(to_heads(query_rows, groups, heads), 'ctx', split_axis=0,...  5.52 us
  transfers between devices with their start and end apart: 28, of which 15 were waited for; matrix products, arithmetic and copies ran while one was open for 12% of the time, Pallas kernels for 0%

commit v1 on v0

--- a/solution.py
+++ b/solution.py
@@ -1,8 +1,11 @@
+import functools
 import math
 
 import jax
 import jax.numpy as jnp
 from jax import lax
+from jax.experimental import pallas as pl
+from jax.experimental.pallas import tpu as pltpu
 from jax.sharding import PartitionSpec as P
 
 
@@ -113,7 +116,7 @@
     return spread.reshape(span_count, groups * slab, heads * width)
 
 
-def per_device(query_rows, key_rows, value_rows, step_rates, gate_weight, up_weight, down_weight):
+def per_device_general(query_rows, key_rows, value_rows, step_rates, gate_weight, up_weight, down_weight):
     heads = step_rates.shape[2]
     span_count = query_rows.shape[0]
     scaled_all = scale_values(value_rows, step_rates)
@@ -179,6 +182,385 @@
     return (from_heads(returned, groups, heads), masters[0], masters[1], masters[2])
 
 
+def mm(left, right, left_dim, right_dim):
+    return lax.dot_general(
+        left,
+        right,
+        (((left_dim,), (right_dim,)), ((), ())),
+        preferred_element_type=jnp.float32,
+    )
+
+
+def sigmoid(values):
+    return 0.5 * jnp.tanh(0.5 * values) + 0.5
+
+
+def fused_kernel(
+    heads,
+    groups,
+    q_ref,
+    k_ref,
+    v_ref,
+    r_ref,
+    gate_ref,
+    up_ref,
+    down_ref,
+    att_ref,
+    gate_out,
+    up_out,
+    down_out,
+    scaled_buf,
+    tok,
+    out_buf,
+    low,
+    low_grad,
+    grad,
+    grad_in,
+    master,
+    total,
+    d_gate,
+    d_up,
+    acts,
+    square,
+    square_in,
+    tok_send,
+    tok_recv,
+    att_send,
+    att_recv,
+    low_send,
+    low_recv,
+    grad_send,
+    grad_recv,
+    square_send,
+    square_recv,
+):
+    spans, count, _ = q_ref.shape
+    rows, width = gate_ref.shape
+    position = lax.axis_index("ctx")
+    head = lax.div(position, groups)
+    member = lax.rem(position, groups)
+
+    def across(step):
+        return lax.rem(head + step, heads)
+
+    def within(step):
+        return lax.rem(member + step, groups)
+
+    def far(which):
+        return {"ctx": which * groups + member}
+
+    def near(which):
+        return {"ctx": head * groups + which}
+
+    def columns(which):
+        return pl.ds(pl.multiple_of(which * width, 128), width)
+
+    def rows_of(which):
+        return pl.ds(pl.multiple_of(which * rows, 16), rows)
+
+    own_rows = rows_of(member)
+    own_columns = columns(head)
+
+    barrier = pltpu.get_barrier_semaphore()
+    for step in range(1, heads):
+        pl.semaphore_signal(
+            barrier, inc=1, device_id=far(across(step)), device_id_type=pl.DeviceIdType.MESH
+        )
+    for step in range(1, groups):
+        pl.semaphore_signal(
+            barrier, inc=1, device_id=near(within(step)), device_id_type=pl.DeviceIdType.MESH
+        )
+
+    def scale(span):
+        for each in range(heads):
+            part = v_ref[span, :, each * width : (each + 1) * width].astype(jnp.float32)
+            rate = r_ref[span, :, each : each + 1]
+            scaled_buf[span, :, each * width : (each + 1) * width] = (part * rate).astype(
+                jnp.bfloat16
+            )
+
+    def token_copy(span, kind, source_at, slot, target):
+        source = (q_ref, k_ref, scaled_buf)[kind]
+        return pltpu.make_async_remote_copy(
+            src_ref=source.at[span, :, columns(source_at)],
+            dst_ref=tok.at[span, kind, slot],
+            send_sem=tok_send.at[span, kind, target],
+            recv_sem=tok_recv.at[span, kind, slot],
+            device_id=far(target),
+            device_id_type=pl.DeviceIdType.MESH,
+        )
+
+    def send_tokens(span, kind):
+        for step in range(1, heads):
+            target = across(step)
+            token_copy(span, kind, target, head, target).start()
+
+    def wait_tokens(span, kind, source):
+        token_copy(span, kind, source, source, source).wait_recv()
+
+    def own_tokens(span, kind):
+        source = (q_ref, k_ref, scaled_buf)[kind]
+        tok[span, kind, head] = source[span, :, own_columns]
+
+    def att_copy(span, slot, column, target):
+        return pltpu.make_async_remote_copy(
+            src_ref=out_buf.at[span, slot],
+            dst_ref=att_ref.at[span, :, columns(column)],
+            send_sem=att_send.at[span, slot],
+            recv_sem=att_recv.at[span, column],
+            device_id=far(target),
+            device_id_type=pl.DeviceIdType.MESH,
+        )
+
+    def low_copy(span, which, block, target):
+        return pltpu.make_async_remote_copy(
+            src_ref=low.at[span, which, rows_of(block)],
+            dst_ref=low.at[span, which, rows_of(block)],
+            send_sem=low_send.at[span, which, target],
+            recv_sem=low_recv.at[span, which, block],
+            device_id=near(target),
+            device_id_type=pl.DeviceIdType.MESH,
+        )
+
+    def grad_copy(span, which, slot, target):
+        return pltpu.make_async_remote_copy(
+            src_ref=low_grad.at[span, which, rows_of(target)],
+            dst_ref=grad_in.at[span, which, slot],
+            send_sem=grad_send.at[span, which, target],
+            recv_sem=grad_recv.at[span, which, slot],
+            device_id=near(target),
+            device_id_type=pl.DeviceIdType.MESH,
+        )
+
+    def square_copy(span, slot, target):
+        return pltpu.make_async_remote_copy(
+            src_ref=square.at[span],
+            dst_ref=square_in.at[span, slot],
+            send_sem=square_send.at[span, target],
+            recv_sem=square_recv.at[span, slot],
+            device_id=near(target),
+            device_id_type=pl.DeviceIdType.MESH,
+        )
+
+    def send_low(span, which):
+        for step in range(1, groups):
+            target = within(step)
+            low_copy(span, which, member, target).start()
+
+    weights = (gate_ref, up_ref, down_ref)
+    finals = (gate_out, up_out, down_out)
+    for which in range(3):
+        low[0, which, own_rows] = weights[which][...].astype(jnp.bfloat16)
+    scale(0)
+    pl.semaphore_wait(barrier, heads + groups - 2)
+    send_tokens(0, 1)
+    send_tokens(0, 2)
+    for which in range(3):
+        send_low(0, which)
+    for span in range(1, spans):
+        scale(span)
+    for span in range(spans):
+        for kind in range(3):
+            own_tokens(span, kind)
+    for span in range(spans):
+        for kind in ((0,) if span == 0 else (1, 2, 0)):
+            send_tokens(span, kind)
+
+    for span in range(spans):
+        for step in range(1, groups):
+            source = within(step)
+            for which in range(3):
+                low_copy(span, which, source, source).wait_recv()
+
+        def forward(step, carry):
+            slot = lax.rem(head + step, heads)
+
+            @pl.when(step > 0)
+            def _():
+                wait_tokens(span, 1, slot)
+                wait_tokens(span, 2, slot)
+
+            keys = tok[span, 1, slot]
+            first = mm(keys, low[span, 0], 1, 1)
+            second = mm(keys, low[span, 1], 1, 1)
+            back = mm(tok[span, 2, slot], low[span, 2], 1, 0)
+            sig = sigmoid(first)
+            silu_first = first * sig
+            slope = sig * (1.0 + first * (1.0 - sig))
+            acts[slot] = (silu_first * second).astype(jnp.bfloat16)
+            d_gate[slot] = (back * second * slope).astype(jnp.bfloat16)
+            d_up[slot] = (back * silu_first).astype(jnp.bfloat16)
+            return carry
+
+        lax.fori_loop(0, heads, forward, 0)
+        keys = tok[span, 1].reshape(heads * count, width)
+        scaled = tok[span, 2].reshape(heads * count, width)
+        pairs = (
+            (d_gate[...].reshape(heads * count, -1), keys),
+            (d_up[...].reshape(heads * count, -1), keys),
+            (scaled, acts[...].reshape(heads * count, -1)),
+        )
+        for which in range(3):
+            product = mm(pairs[which][0], pairs[which][1], 0, 0)
+            grad[which] = product
+            low_grad[span, which] = product.astype(jnp.bfloat16)
+            for step in range(1, groups):
+                target = within(step)
+                grad_copy(span, which, member, target).start()
+
+        def answer(step, carry):
+            slot = lax.rem(head + step, heads)
+
+            @pl.when(step > 0)
+            def _():
+                wait_tokens(span, 0, slot)
+
+            queries = tok[span, 0, slot]
+            first = mm(queries, low[span, 0], 1, 1)
+            second = mm(queries, low[span, 1], 1, 1)
+            hidden = (first * sigmoid(first) * second).astype(jnp.bfloat16)
+            out_buf[span, slot] = mm(hidden, low[span, 2], 1, 1).astype(jnp.bfloat16)
+
+            @pl.when(step > 0)
+            def _():
+                att_copy(span, slot, head, slot).start()
+
+            return carry
+
+        def collect():
+            for which in range(3):
+                summed = grad[which, own_rows]
+                for step in range(1, groups):
+                    source = within(step)
+                    grad_copy(span, which, source, source).wait_recv()
+                    summed = summed + grad_in[span, which, source].astype(jnp.float32)
+                total[which] = summed
+                squared = summed * summed
+                by_row = jnp.sum(squared.reshape(rows // 8, 8, width), axis=0)
+                lanes = by_row[:, :128]
+                for at in range(128, width, 128):
+                    lanes = lanes + by_row[:, at : at + 128]
+                square[span, which] = lanes
+            for step in range(1, groups):
+                square_copy(span, member, within(step)).start()
+
+        def refresh():
+            for step in range(1, groups):
+                source = within(step)
+                square_copy(span, source, source).wait_recv()
+            for which in range(3):
+                sums = square[span, which]
+                for step in range(1, groups):
+                    sums = sums + square_in[span, within(step), which]
+                block_mean = jnp.sum(sums, keepdims=True) / (rows * groups * width)
+                factor = lax.rsqrt(block_mean + 1e-06) / math.sqrt(width)
+                before = weights[which][...] if span == 0 else master[which]
+                stepped = before + total[which] * factor
+                row_mean = jnp.mean(stepped * stepped, axis=1, keepdims=True)
+                after = stepped * (lax.rsqrt(row_mean + 1e-06) / math.sqrt(width))
+                if span == spans - 1:
+                    finals[which][...] = after
+                else:
+                    master[which] = after
+                    low[span + 1, which, own_rows] = after.astype(jnp.bfloat16)
+                    send_low(span + 1, which)
+
+        lax.fori_loop(0, heads, answer, 0)
+        collect()
+        refresh()
+        att_ref[span, :, own_columns] = out_buf[span, head]
+
+    for span in range(spans):
+        for step in range(1, heads):
+            other = across(step)
+            att_copy(span, other, other, other).wait_recv()
+            att_copy(span, other, other, other).wait_send()
+            for kind in range(3):
+                token_copy(span, kind, other, other, other).wait_send()
+        for step in range(1, groups):
+            other = within(step)
+            for which in range(3):
+                low_copy(span, which, other, other).wait_send()
+                grad_copy(span, which, other, other).wait_send()
+            square_copy(span, other, other).wait_send()
+
+
+def per_device_fused(
+    heads, groups, query_rows, key_rows, value_rows, step_rates, gate_weight, up_weight, down_weight
+):
+    spans, count, full = query_rows.shape
+    rows, width = gate_weight.shape
+    block = rows * groups
+    low = jnp.bfloat16
+    vmem = pl.BlockSpec(memory_space=pltpu.VMEM)
+    weight = jax.ShapeDtypeStruct((rows, width), jnp.float32)
+    dma = pltpu.SemaphoreType.DMA
+    return pl.pallas_call(
+        functools.partial(fused_kernel, heads, groups),
+        out_shape=(
+            jax.ShapeDtypeStruct((spans, count, full), low),
+            weight,
+            weight,
+            weight,
+        ),
+        in_specs=[vmem] * 7,
+        out_specs=(vmem,) * 4,
+        scratch_shapes=[
+            pltpu.VMEM((spans, count, full), low),
+            pltpu.VMEM((spans, 3, heads, count, width), low),
+            pltpu.VMEM((spans, heads, count, width), low),
+            pltpu.VMEM((spans, 3, block, width), low),
+            pltpu.VMEM((spans, 3, block, width), low),
+            pltpu.VMEM((3, block, width), jnp.float32),
+            pltpu.VMEM((spans, 3, groups, rows, width), low),
+            pltpu.VMEM((3, rows, width), jnp.float32),
+            pltpu.VMEM((3, rows, width), jnp.float32),
+            pltpu.VMEM((heads, count, width), low),
+            pltpu.VMEM((heads, count, width), low),
+            pltpu.VMEM((heads, count, width), low),
+            pltpu.VMEM((spans, 3, 8, 128), jnp.float32),
+            pltpu.VMEM((spans, groups, 3, 8, 128), jnp.float32),
+            dma((spans, 3, heads)),
+            dma((spans, 3, heads)),
+            dma((spans, heads)),
+            dma((spans, heads)),
+            dma((spans, 3, groups)),
+            dma((spans, 3, groups)),
+            dma((spans, 3, groups)),
+            dma((spans, 3, groups)),
+            dma((spans, groups)),
+            dma((spans, groups)),
+        ],
+        compiler_params=pltpu.CompilerParams(
+            collective_id=0, has_side_effects=True, vmem_limit_bytes=40 * 2**20
+        ),
+    )(query_rows, key_rows, value_rows, step_rates, gate_weight, up_weight, down_weight)
+
+
+def per_device(query_rows, key_rows, value_rows, step_rates, gate_weight, up_weight, down_weight):
+    arguments = (
+        query_rows, key_rows, value_rows, step_rates, gate_weight, up_weight, down_weight
+    )
+    heads = step_rates.shape[2]
+    size = lax.axis_size("ctx")
+    rows, width = gate_weight.shape
+    count = query_rows.shape[1]
+    groups = size // heads
+    fits = (
+        size % heads == 0
+        and down_weight.shape == gate_weight.shape
+        and rows * groups == width
+        and query_rows.shape[2] == heads * width
+        and rows % 16 == 0
+        and width % 128 == 0
+        and count % 16 == 0
+        and 2 <= groups <= 8
+    )
+    if fits:
+        return per_device_fused(heads, groups, *arguments)
+    return per_device_general(*arguments)
+
+
 def solution(mesh):
     placed = (
         P(None, ("parts", "ctx"), None),

time: 231 us -> 86.9 us (0.38)
  the two profiles are of different devices: /device:TPU:0 before, /device:TPU:9 now
where the time goes in v1:
time: 86.9 us; the launch traced here: 86.6 us
  Pallas kernels  76.1 us (88%)
  local copies, waits for them, and re-layouts  9.8 us (11%)
    pallas_call x1, Pallas kernels, per_device_fused(): pl.pallas_call(functools.partial(fused_kernel, heads, groups), out_shape=...  76.1 us
    unnamed x17, local copies, waits for them, and re-layouts  9.8 us

profile of v1, /device:TPU:9, one launch (start us, length us, event | category | flops | bytes accessed | tf_op | source)
XLA Modules:
  0.0 86.6 jit_solution(15338227797283070383)
XLA Ops:
  0.6 0.8 copy.11.r_ref
  1.5 0.0 copy-start
  1.5 1.1 %copy-done = bf16[2,128,1536]{2,1,0:T(8,128)(2,1)S(1)} copy-done((bf16[2,128,1536]{2,1,0:T(8,128)(2,1)S(1)}, bf16[2,128,1536]{2,1,0:T(8,128)(2,1)}, u32[]{:S(2)}) %copy-start) | copy-done | bytes 786456
  2.6 0.0 copy-start.1
  2.6 1.1 %copy-done.1 = bf16[2,128,1536]{2,1,0:T(8,128)(2,1)S(1)} copy-done((bf16[2,128,1536]{2,1,0:T(8,128)(2,1)S(1)}, bf16[2,128,1536]{2,1,0:T(8,128)(2,1)}, u32[]{:S(2)}) %copy-start.1) | copy-done | bytes 786456
  3.7 0.0 copy-start.2
  3.7 1.1 %copy-done.2 = bf16[2,128,1536]{2,1,0:T(8,128)(2,1)S(1)} copy-done((bf16[2,128,1536]{2,1,0:T(8,128)(2,1)S(1)}, bf16[2,128,1536]{2,1,0:T(8,128)(2,1)}, u32[]{:S(2)}) %copy-start.2) | copy-done | bytes 786456
  4.9 0.0 copy-start.3
  4.9 0.9 %copy-done.3 = f32[96,384]{1,0:T(8,128)S(1)} copy-done((f32[96,384]{1,0:T(8,128)S(1)}, f32[96,384]{1,0:T(8,128)}, u32[]{:S(2)}) %copy-start.3) | copy-done | bytes 147480
  5.8 0.0 copy-start.4
  5.8 0.9 %copy-done.4 = f32[96,384]{1,0:T(8,128)S(1)} copy-done((f32[96,384]{1,0:T(8,128)S(1)}, f32[96,384]{1,0:T(8,128)}, u32[]{:S(2)}) %copy-start.4) | copy-done | bytes 147480
  6.7 0.0 copy-start.5
  6.7 0.9 %copy-done.5 = f32[96,384]{1,0:T(8,128)S(1)} copy-done((f32[96,384]{1,0:T(8,128)S(1)}, f32[96,384]{1,0:T(8,128)}, u32[]{:S(2)}) %copy-start.5) | copy-done | bytes 147480
  7.6 76.1 %shard_map.102 = (bf16[2,128,1536]{2,1,0:T(8,128)(2,1)S(1)}, f32[96,384]{1,0:T(8,128)S(1)}, f32[96,384]{1,0:T(8,128)S(1)}, f32[96,384]{1,0:T(8,128)S(1)}) custom-call(bf16[2,128,1536]{2,1,0:T(8,128)(2,1)S(1)} %copy-done, bf16[2,128,1536]{2,1,0:T(8,128)(2,1)S(1)} %copy-done.1, bf16[2,128,1536]{2,1,0:T(8,128)(2,1)S(1)} %copy-done.2, ...), custom_call_target="tpu_custom_call" | custom-call | tf_op jit(solution)/shard_map/pallas_call | solution.py:498
  83.7 0.9 %copy.16 = bf16[2,128,1536]{2,1,0:T(8,128)(2,1)} copy(bf16[2,128,1536]{2,1,0:T(8,128)(2,1)S(1)} %get-tuple-element.8) | data formatting | bytes 1572864
  84.6 0.7 copy.17
  85.2 0.7 copy.18
  85.9 0.7 copy.19
Async XLA Ops:
  1.5 1.1 %copy-start = (bf16[2,128,1536]{2,1,0:T(8,128)(2,1)S(1)}, bf16[2,128,1536]{2,1,0:T(8,128)(2,1)}, u32[]{:S(2)}) copy-start(bf16[2,128,1536]{2,1,0:T(8,128)(2,1)} %q_ref.1) | copy-start | bytes 2359300
  2.6 1.1 %copy-start.1 = (bf16[2,128,1536]{2,1,0:T(8,128)(2,1)S(1)}, bf16[2,128,1536]{2,1,0:T(8,128)(2,1)}, u32[]{:S(2)}) copy-start(bf16[2,128,1536]{2,1,0:T(8,128)(2,1)} %k_ref.1) | copy-start | bytes 2359300
  3.7 1.1 %copy-start.2 = (bf16[2,128,1536]{2,1,0:T(8,128)(2,1)S(1)}, bf16[2,128,1536]{2,1,0:T(8,128)(2,1)}, u32[]{:S(2)}) copy-start(bf16[2,128,1536]{2,1,0:T(8,128)(2,1)} %v_ref.1) | copy-start | bytes 2359300
  4.9 0.9 %copy-start.3 = (f32[96,384]{1,0:T(8,128)S(1)}, f32[96,384]{1,0:T(8,128)}, u32[]{:S(2)}) copy-start(f32[96,384]{1,0:T(8,128)} %gate_ref.1) | copy-start | bytes 442372
  5.8 0.9 %copy-start.4 = (f32[96,384]{1,0:T(8,128)S(1)}, f32[96,384]{1,0:T(8,128)}, u32[]{:S(2)}) copy-start(f32[96,384]{1,0:T(8,128)} %up_ref.1) | copy-start | bytes 442372
  6.7 0.9 %copy-start.5 = (f32[96,384]{1,0:T(8,128)S(1)}, f32[96,384]{1,0:T(8,128)}, u32[]{:S(2)}) copy-start(f32[96,384]{1,0:T(8,128)} %down_ref.1) | copy-start | bytes 442372

commit v2 on v1

--- a/solution.py
+++ b/solution.py
@@ -182,6 +182,9 @@
     return (from_heads(returned, groups, heads), masters[0], masters[1], masters[2])
 
 
+PIECES = 2
+
+
 def mm(left, right, left_dim, right_dim):
     return lax.dot_general(
         left,
@@ -211,6 +214,7 @@
     down_out,
     scaled_buf,
     tok,
+    tok_query,
     out_buf,
     low,
     low_grad,
@@ -225,8 +229,12 @@
     square_in,
     tok_send,
     tok_recv,
+    query_send,
+    query_recv,
     att_send,
     att_recv,
+    chain_send,
+    chain_recv,
     low_send,
     low_recv,
     grad_send,
@@ -240,6 +248,16 @@
     head = lax.div(position, groups)
     member = lax.rem(position, groups)
 
+    half = heads // 2
+    piece = low.shape[3] // PIECES
+
+    def query_head(which):
+        return lax.rem(which, 2) * half + lax.div(which, 2)
+
+    quest = query_head(member)
+    apart = (head - quest) * (head - quest)
+    held = lax.div(apart + heads * heads - 1, heads * heads)
+
     def across(step):
         return lax.rem(head + step, heads)
 
@@ -280,7 +298,7 @@
             )
 
     def token_copy(span, kind, source_at, slot, target):
-        source = (q_ref, k_ref, scaled_buf)[kind]
+        source = (k_ref, scaled_buf)[kind]
         return pltpu.make_async_remote_copy(
             src_ref=source.at[span, :, columns(source_at)],
             dst_ref=tok.at[span, kind, slot],
@@ -299,23 +317,97 @@
         token_copy(span, kind, source, source, source).wait_recv()
 
     def own_tokens(span, kind):
-        source = (q_ref, k_ref, scaled_buf)[kind]
+        source = (k_ref, scaled_buf)[kind]
         tok[span, kind, head] = source[span, :, own_columns]
 
-    def att_copy(span, slot, column, target):
+    def query_copy(span, column, slot, target):
+        return pltpu.make_async_remote_copy(
+            src_ref=q_ref.at[span, :, columns(column)],
+            dst_ref=tok_query.at[span, slot],
+            send_sem=query_send.at[span, target],
+            recv_sem=query_recv.at[span, slot],
+            device_id=near(target),
+            device_id_type=pl.DeviceIdType.MESH,
+        )
+
+    def send_queries(span):
+        for step in range(1, groups):
+            target = within(step)
+            query_copy(span, query_head(target), member, target).start()
+
+    def att_copy(span, slot, column, source, target):
         return pltpu.make_async_remote_copy(
             src_ref=out_buf.at[span, slot],
             dst_ref=att_ref.at[span, :, columns(column)],
             send_sem=att_send.at[span, slot],
-            recv_sem=att_recv.at[span, column],
+            recv_sem=att_recv.at[span, source],
+            device_id=near(target),
+            device_id_type=pl.DeviceIdType.MESH,
+        )
+
+    def send_att(span):
+        for step in range(1, groups):
+            target = within(step)
+            att_copy(span, target, quest, member, target).start()
+
+    def chain_copy(span, which, part, side, target):
+        cut = pl.ds(part * piece, piece)
+        return pltpu.make_async_remote_copy(
+            src_ref=low.at[span, held, which, cut],
+            dst_ref=low.at[span, 1, which, cut],
+            send_sem=chain_send.at[span, which, part, side],
+            recv_sem=chain_recv.at[span, which, part],
             device_id=far(target),
             device_id_type=pl.DeviceIdType.MESH,
         )
 
+    def chain_start(span, which):
+        @pl.when(head == quest)
+        def _():
+            for part in range(PIECES):
+
+                @pl.when(head < heads - 1)
+                def _():
+                    chain_copy(span, which, part, 0, head + 1).start()
+
+                @pl.when(head > 0)
+                def _():
+                    chain_copy(span, which, part, 1, head - 1).start()
+
+    def chain_pass(span, which):
+        for part in range(PIECES):
+
+            @pl.when(head > quest)
+            def _():
+                chain_copy(span, which, part, 0, head - 1).wait_recv()
+
+                @pl.when(head < heads - 1)
+                def _():
+                    chain_copy(span, which, part, 0, head + 1).start()
+
+            @pl.when(head < quest)
+            def _():
+                chain_copy(span, which, part, 1, head + 1).wait_recv()
+
+                @pl.when(head > 0)
+                def _():
+                    chain_copy(span, which, part, 1, head - 1).start()
+
+    def chain_finish(span, which):
+        for part in range(PIECES):
+
+            @pl.when((head >= quest) & (head < heads - 1))
+            def _():
+                chain_copy(span, which, part, 0, head + 1).wait_send()
+
+            @pl.when((head <= quest) & (head > 0))
+            def _():
+                chain_copy(span, which, part, 1, head - 1).wait_send()
+
     def low_copy(span, which, block, target):
         return pltpu.make_async_remote_copy(
-            src_ref=low.at[span, which, rows_of(block)],
-            dst_ref=low.at[span, which, rows_of(block)],
+            src_ref=low.at[span, 0, which, rows_of(block)],
+            dst_ref=low.at[span, 0, which, rows_of(block)],
             send_sem=low_send.at[span, which, target],
             recv_sem=low_recv.at[span, which, block],
             device_id=near(target),
@@ -350,40 +442,44 @@
     weights = (gate_ref, up_ref, down_ref)
     finals = (gate_out, up_out, down_out)
     for which in range(3):
-        low[0, which, own_rows] = weights[which][...].astype(jnp.bfloat16)
+        low[0, 0, which, own_rows] = weights[which][...].astype(jnp.bfloat16)
     scale(0)
     pl.semaphore_wait(barrier, heads + groups - 2)
+    send_tokens(0, 0)
     send_tokens(0, 1)
-    send_tokens(0, 2)
     for which in range(3):
         send_low(0, which)
+    for span in range(spans):
+        send_queries(span)
     for span in range(1, spans):
         scale(span)
     for span in range(spans):
-        for kind in range(3):
+        for kind in range(2):
             own_tokens(span, kind)
+        tok_query[span, member] = q_ref[span, :, columns(quest)]
+
     for span in range(spans):
-        for kind in ((0,) if span == 0 else (1, 2, 0)):
-            send_tokens(span, kind)
-
-    for span in range(spans):
-        for step in range(1, groups):
-            source = within(step)
-            for which in range(3):
+        for which in range(3):
+            for step in range(1, groups):
+                source = within(step)
                 low_copy(span, which, source, source).wait_recv()
+            if span > 0:
+                chain_start(span, which)
+        if span > 0:
+            send_att(span - 1)
 
         def forward(step, carry):
             slot = lax.rem(head + step, heads)
 
             @pl.when(step > 0)
             def _():
+                wait_tokens(span, 0, slot)
                 wait_tokens(span, 1, slot)
-                wait_tokens(span, 2, slot)
-
-            keys = tok[span, 1, slot]
-            first = mm(keys, low[span, 0], 1, 1)
-            second = mm(keys, low[span, 1], 1, 1)
-            back = mm(tok[span, 2, slot], low[span, 2], 1, 0)
+
+            keys = tok[span, 0, slot]
+            first = mm(keys, low[span, 0, 0], 1, 1)
+            second = mm(keys, low[span, 0, 1], 1, 1)
+            back = mm(tok[span, 1, slot], low[span, 0, 2], 1, 0)
             sig = sigmoid(first)
             silu_first = first * sig
             slope = sig * (1.0 + first * (1.0 - sig))
@@ -393,8 +489,11 @@
             return carry
 
         lax.fori_loop(0, heads, forward, 0)
-        keys = tok[span, 1].reshape(heads * count, width)
-        scaled = tok[span, 2].reshape(heads * count, width)
+        if span == 0:
+            for which in range(3):
+                chain_start(span, which)
+        keys = tok[span, 0].reshape(heads * count, width)
+        scaled = tok[span, 1].reshape(heads * count, width)
         pairs = (
             (d_gate[...].reshape(heads * count, -1), keys),
             (d_up[...].reshape(heads * count, -1), keys),
@@ -408,22 +507,29 @@
                 target = within(step)
                 grad_copy(span, which, member, target).start()
 
+        for which in range(3):
+            chain_pass(span, which)
+        if span + 1 < spans:
+            for kind in range(2):
+                send_tokens(span + 1, kind)
+
         def answer(step, carry):
-            slot = lax.rem(head + step, heads)
+            slot = lax.rem(member + step, groups)
 
             @pl.when(step > 0)
             def _():
-                wait_tokens(span, 0, slot)
-
-            queries = tok[span, 0, slot]
-            first = mm(queries, low[span, 0], 1, 1)
-            second = mm(queries, low[span, 1], 1, 1)
+                query_copy(span, head, slot, slot).wait_recv()
+
+            queries = tok_query[span, slot]
+            first = mm(queries, low[span, held, 0], 1, 1)
+            second = mm(queries, low[span, held, 1], 1, 1)
             hidden = (first * sigmoid(first) * second).astype(jnp.bfloat16)
-            out_buf[span, slot] = mm(hidden, low[span, 2], 1, 1).astype(jnp.bfloat16)
-
-            @pl.when(step > 0)
-            def _():
-                att_copy(span, slot, head, slot).start()
+            out_buf[span, slot] = mm(hidden, low[span, held, 2], 1, 1).astype(jnp.bfloat16)
+            if span == spans - 1:
+
+                @pl.when(step > 0)
+                def _():
+                    att_copy(span, slot, quest, member, slot).start()
 
             return carry
 
@@ -462,21 +568,29 @@
                     finals[which][...] = after
                 else:
                     master[which] = after
-                    low[span + 1, which, own_rows] = after.astype(jnp.bfloat16)
+                    low[span + 1, 0, which, own_rows] = after.astype(jnp.bfloat16)
                     send_low(span + 1, which)
 
-        lax.fori_loop(0, heads, answer, 0)
         collect()
-        refresh()
-        att_ref[span, :, own_columns] = out_buf[span, head]
+        if span + 1 < spans:
+            refresh()
+        lax.fori_loop(0, groups, answer, 0)
+        att_ref[span, :, columns(quest)] = out_buf[span, member]
+        if span + 1 == spans:
+            refresh()
 
     for span in range(spans):
         for step in range(1, heads):
             other = across(step)
-            att_copy(span, other, other, other).wait_recv()
-            att_copy(span, other, other, other).wait_send()
-            for kind in range(3):
+            for kind in range(2):
                 token_copy(span, kind, other, other, other).wait_send()
+        for which in range(3):
+            chain_finish(span, which)
+        for step in range(1, groups):
+            other = within(step)
+            att_copy(span, other, query_head(other), other, other).wait_recv()
+            att_copy(span, other, quest, member, other).wait_send()
+            query_copy(span, query_head(other), member, other).wait_send()
         for step in range(1, groups):
             other = within(step)
             for which in range(3):
@@ -507,9 +621,10 @@
         out_specs=(vmem,) * 4,
         scratch_shapes=[
             pltpu.VMEM((spans, count, full), low),
-            pltpu.VMEM((spans, 3, heads, count, width), low),
-            pltpu.VMEM((spans, heads, count, width), low),
-            pltpu.VMEM((spans, 3, block, width), low),
+            pltpu.VMEM((spans, 2, heads, count, width), low),
+            pltpu.VMEM((spans, groups, count, width), low),
+            pltpu.VMEM((spans, groups, count, width), low),
+            pltpu.VMEM((spans, 2, 3, block, width), low),
             pltpu.VMEM((spans, 3, block, width), low),
             pltpu.VMEM((3, block, width), jnp.float32),
             pltpu.VMEM((spans, 3, groups, rows, width), low),
@@ -520,10 +635,14 @@
             pltpu.VMEM((heads, count, width), low),
             pltpu.VMEM((spans, 3, 8, 128), jnp.float32),
             pltpu.VMEM((spans, groups, 3, 8, 128), jnp.float32),
-            dma((spans, 3, heads)),
-            dma((spans, 3, heads)),
-            dma((spans, heads)),
-            dma((spans, heads)),
+            dma((spans, 2, heads)),
+            dma((spans, 2, heads)),
+            dma((spans, groups)),
+            dma((spans, groups)),
+            dma((spans, groups)),
+            dma((spans, groups)),
+            dma((spans, 3, PIECES, 2)),
+            dma((spans, 3, PIECES)),
             dma((spans, 3, groups)),
             dma((spans, 3, groups)),
             dma((spans, 3, groups)),
@@ -554,7 +673,9 @@
         and rows % 16 == 0
         and width % 128 == 0
         and count % 16 == 0
-        and 2 <= groups <= 8
+        and groups == heads
+        and heads % 2 == 0
+        and width % (16 * PIECES) == 0
     )
     if fits:
         return per_device_fused(heads, groups, *arguments)

time: 86.9 us -> 106 us (1.22)
  the two profiles are of different devices: /device:TPU:9 before, /device:TPU:0 now
where the time goes in v2:
time: 106 us; the launch traced here: 105 us
  Pallas kernels  94.7 us (89%)
  local copies, waits for them, and re-layouts  9.8 us (9%)
    pallas_call x1, Pallas kernels, per_device_fused(): pl.pallas_call(functools.partial(fused_kernel, heads, groups), out_shape=...  94.7 us
    unnamed x17, local copies, waits for them, and re-layouts  9.8 us

profile of v2, /device:TPU:0, one launch (start us, length us, event | category | flops | bytes accessed | tf_op | source)
XLA Modules:
  0.0 105.2 jit_solution(3414924981497469569)
XLA Ops:
  0.6 0.8 copy.11.r_ref
  1.5 0.0 copy-start
  1.5 1.1 %copy-done = bf16[2,128,1536]{2,1,0:T(8,128)(2,1)S(1)} copy-done((bf16[2,128,1536]{2,1,0:T(8,128)(2,1)S(1)}, bf16[2,128,1536]{2,1,0:T(8,128)(2,1)}, u32[]{:S(2)}) %copy-start) | copy-done | bytes 786456
  2.6 0.0 copy-start.1
  2.6 1.1 %copy-done.1 = bf16[2,128,1536]{2,1,0:T(8,128)(2,1)S(1)} copy-done((bf16[2,128,1536]{2,1,0:T(8,128)(2,1)S(1)}, bf16[2,128,1536]{2,1,0:T(8,128)(2,1)}, u32[]{:S(2)}) %copy-start.1) | copy-done | bytes 786456
  3.7 0.0 copy-start.2
  3.7 1.1 %copy-done.2 = bf16[2,128,1536]{2,1,0:T(8,128)(2,1)S(1)} copy-done((bf16[2,128,1536]{2,1,0:T(8,128)(2,1)S(1)}, bf16[2,128,1536]{2,1,0:T(8,128)(2,1)}, u32[]{:S(2)}) %copy-start.2) | copy-done | bytes 786456
  4.9 0.0 copy-start.3
  4.9 0.9 copy-done.3
  5.8 0.0 copy-start.4
  5.8 0.9 copy-done.4
  6.7 0.0 copy-start.5
  6.7 0.9 copy-done.5
  7.6 94.7 %shard_map.102 = (bf16[2,128,1536]{2,1,0:T(8,128)(2,1)S(1)}, f32[96,384]{1,0:T(8,128)S(1)}, f32[96,384]{1,0:T(8,128)S(1)}, f32[96,384]{1,0:T(8,128)S(1)}) custom-call(bf16[2,128,1536]{2,1,0:T(8,128)(2,1)S(1)} %copy-done, bf16[2,128,1536]{2,1,0:T(8,128)(2,1)S(1)} %copy-done.1, bf16[2,128,1536]{2,1,0:T(8,128)(2,1)S(1)} %copy-done.2, ...), custom_call_target="tpu_custom_call" | custom-call | tf_op jit(solution)/shard_map/pallas_call | solution.py:612
  102.3 0.9 copy.16
  103.2 0.7 copy.17
  103.9 0.7 copy.18
  104.5 0.7 copy.19
Async XLA Ops:
  1.5 1.1 %copy-start = (bf16[2,128,1536]{2,1,0:T(8,128)(2,1)S(1)}, bf16[2,128,1536]{2,1,0:T(8,128)(2,1)}, u32[]{:S(2)}) copy-start(bf16[2,128,1536]{2,1,0:T(8,128)(2,1)} %q_ref.1) | copy-start | bytes 2359300
  2.6 1.1 %copy-start.1 = (bf16[2,128,1536]{2,1,0:T(8,128)(2,1)S(1)}, bf16[2,128,1536]{2,1,0:T(8,128)(2,1)}, u32[]{:S(2)}) copy-start(bf16[2,128,1536]{2,1,0:T(8,128)(2,1)} %k_ref.1) | copy-start | bytes 2359300
  3.7 1.1 %copy-start.2 = (bf16[2,128,1536]{2,1,0:T(8,128)(2,1)S(1)}, bf16[2,128,1536]{2,1,0:T(8,128)(2,1)}, u32[]{:S(2)}) copy-start(bf16[2,128,1536]{2,1,0:T(8,128)(2,1)} %v_ref.1) | copy-start | bytes 2359300
  4.9 0.9 copy-start.3
  5.8 0.9 copy-start.4
  6.7 0.9 copy-start.5

commit v3 on v1

--- a/solution.py
+++ b/solution.py
@@ -215,6 +215,8 @@
     low,
     low_grad,
     grad,
+    mate_in,
+    pair_sum,
     grad_in,
     master,
     total,
@@ -229,6 +231,8 @@
     att_recv,
     low_send,
     low_recv,
+    mate_send,
+    mate_recv,
     grad_send,
     grad_recv,
     square_send,
@@ -240,6 +244,14 @@
     head = lax.div(position, groups)
     member = lax.rem(position, groups)
 
+    side = lax.rem(member, 2)
+    pair = lax.div(member, 2)
+    mate = member + 1 - 2 * side
+    pairs_here = groups // 2
+
+    def alike(step):
+        return lax.rem(member + 2 * step, groups)
+
     def across(step):
         return lax.rem(head + step, heads)
 
@@ -312,23 +324,33 @@
             device_id_type=pl.DeviceIdType.MESH,
         )
 
-    def low_copy(span, which, block, target):
+    def low_copy(span, which, block, target, relay):
         return pltpu.make_async_remote_copy(
             src_ref=low.at[span, which, rows_of(block)],
             dst_ref=low.at[span, which, rows_of(block)],
-            send_sem=low_send.at[span, which, target],
+            send_sem=low_send.at[span, which, relay, block if relay else target],
             recv_sem=low_recv.at[span, which, block],
             device_id=near(target),
             device_id_type=pl.DeviceIdType.MESH,
         )
 
+    def mate_copy(span, which):
+        return pltpu.make_async_remote_copy(
+            src_ref=low_grad.at[span, which, 1 - side],
+            dst_ref=mate_in.at[span, which],
+            send_sem=mate_send.at[span, which],
+            recv_sem=mate_recv.at[span, which],
+            device_id=near(mate),
+            device_id_type=pl.DeviceIdType.MESH,
+        )
+
     def grad_copy(span, which, slot, target):
         return pltpu.make_async_remote_copy(
-            src_ref=low_grad.at[span, which, rows_of(target)],
+            src_ref=pair_sum.at[span, which, target],
             dst_ref=grad_in.at[span, which, slot],
             send_sem=grad_send.at[span, which, target],
             recv_sem=grad_recv.at[span, which, slot],
-            device_id=near(target),
+            device_id=near(2 * target + side),
             device_id_type=pl.DeviceIdType.MESH,
         )
 
@@ -343,9 +365,23 @@
         )
 
     def send_low(span, which):
-        for step in range(1, groups):
-            target = within(step)
-            low_copy(span, which, member, target).start()
+        for step in range(1, pairs_here):
+            low_copy(span, which, member, alike(step), 0).start()
+        low_copy(span, which, member, mate, 0).start()
+
+    def gather_low(span):
+        for which in range(3):
+            for step in range(1, pairs_here):
+                other = alike(step)
+                low_copy(span, which, other, other, 0).wait_recv()
+                low_copy(span, which, other, mate, 1).start()
+
+    def finish_low(span):
+        for which in range(3):
+            low_copy(span, which, mate, mate, 0).wait_recv()
+            for step in range(1, pairs_here):
+                other = alike(step) + mate - member
+                low_copy(span, which, other, mate, 1).wait_recv()
 
     weights = (gate_ref, up_ref, down_ref)
     finals = (gate_out, up_out, down_out)
@@ -363,36 +399,43 @@
         for kind in range(3):
             own_tokens(span, kind)
     for span in range(spans):
-        for kind in ((0,) if span == 0 else (1, 2, 0)):
-            send_tokens(span, kind)
-
-    for span in range(spans):
-        for step in range(1, groups):
-            source = within(step)
-            for which in range(3):
-                low_copy(span, which, source, source).wait_recv()
+        gather_low(span)
+        finish_low(span)
 
         def forward(step, carry):
-            slot = lax.rem(head + step, heads)
-
-            @pl.when(step > 0)
-            def _():
-                wait_tokens(span, 1, slot)
-                wait_tokens(span, 2, slot)
-
-            keys = tok[span, 1, slot]
+            duo = lax.rem(lax.div(head, 2) + step, heads // 2)
+            for at in range(2):
+                slot = 2 * duo + at
+
+                @pl.when(slot != head)
+                def _():
+                    wait_tokens(span, 1, slot)
+                    wait_tokens(span, 2, slot)
+
+            if span == 0:
+
+                @pl.when(step == heads // 2 - 1)
+                def _():
+                    for later in range(1, spans):
+                        send_tokens(later, 1)
+                        send_tokens(later, 2)
+                    for later in range(spans):
+                        send_tokens(later, 0)
+
+            keys = tok[span, 1, pl.ds(2 * duo, 2)].reshape(2 * count, width)
             first = mm(keys, low[span, 0], 1, 1)
             second = mm(keys, low[span, 1], 1, 1)
-            back = mm(tok[span, 2, slot], low[span, 2], 1, 0)
+            sent = tok[span, 2, pl.ds(2 * duo, 2)].reshape(2 * count, width)
+            back = mm(sent, low[span, 2], 1, 0)
             sig = sigmoid(first)
             silu_first = first * sig
             slope = sig * (1.0 + first * (1.0 - sig))
-            acts[slot] = (silu_first * second).astype(jnp.bfloat16)
-            d_gate[slot] = (back * second * slope).astype(jnp.bfloat16)
-            d_up[slot] = (back * silu_first).astype(jnp.bfloat16)
+            acts[duo] = (silu_first * second).astype(jnp.bfloat16)
+            d_gate[duo] = (back * second * slope).astype(jnp.bfloat16)
+            d_up[duo] = (back * silu_first).astype(jnp.bfloat16)
             return carry
 
-        lax.fori_loop(0, heads, forward, 0)
+        lax.fori_loop(0, heads // 2, forward, 0)
         keys = tok[span, 1].reshape(heads * count, width)
         scaled = tok[span, 2].reshape(heads * count, width)
         pairs = (
@@ -403,35 +446,51 @@
         for which in range(3):
             product = mm(pairs[which][0], pairs[which][1], 0, 0)
             grad[which] = product
-            low_grad[span, which] = product.astype(jnp.bfloat16)
-            for step in range(1, groups):
-                target = within(step)
-                grad_copy(span, which, member, target).start()
+            lowered = product.astype(jnp.bfloat16)
+            for each in range(groups):
+                low_grad[span, which, each % 2, each // 2] = lowered[
+                    each * rows : (each + 1) * rows
+                ]
+            mate_copy(span, which).start()
+        for which in range(3):
+            mate_copy(span, which).wait_recv()
+            for step in range(1, pairs_here):
+                other = lax.div(alike(step), 2)
+                pair_sum[span, which, other] = (
+                    grad[which, rows_of(alike(step))]
+                    + mate_in[span, which, other].astype(jnp.float32)
+                ).astype(jnp.bfloat16)
+                grad_copy(span, which, pair, other).start()
 
         def answer(step, carry):
-            slot = lax.rem(head + step, heads)
-
-            @pl.when(step > 0)
-            def _():
-                wait_tokens(span, 0, slot)
-
-            queries = tok[span, 0, slot]
+            duo = lax.rem(lax.div(head, 2) + step, heads // 2)
+            for at in range(2):
+                slot = 2 * duo + at
+
+                @pl.when(slot != head)
+                def _():
+                    wait_tokens(span, 0, slot)
+
+            queries = tok[span, 0, pl.ds(2 * duo, 2)].reshape(2 * count, width)
             first = mm(queries, low[span, 0], 1, 1)
             second = mm(queries, low[span, 1], 1, 1)
             hidden = (first * sigmoid(first) * second).astype(jnp.bfloat16)
-            out_buf[span, slot] = mm(hidden, low[span, 2], 1, 1).astype(jnp.bfloat16)
-
-            @pl.when(step > 0)
-            def _():
-                att_copy(span, slot, head, slot).start()
+            answers = mm(hidden, low[span, 2], 1, 1).astype(jnp.bfloat16)
+            for at in range(2):
+                slot = 2 * duo + at
+                out_buf[span, slot] = answers[at * count : (at + 1) * count]
+
+                @pl.when(slot != head)
+                def _():
+                    att_copy(span, slot, head, slot).start()
 
             return carry
 
         def collect():
             for which in range(3):
-                summed = grad[which, own_rows]
-                for step in range(1, groups):
-                    source = within(step)
+                summed = grad[which, own_rows] + mate_in[span, which, pair].astype(jnp.float32)
+                for step in range(1, pairs_here):
+                    source = lax.div(alike(step), 2)
                     grad_copy(span, which, source, source).wait_recv()
                     summed = summed + grad_in[span, which, source].astype(jnp.float32)
                 total[which] = summed
@@ -465,9 +524,13 @@
                     low[span + 1, which, own_rows] = after.astype(jnp.bfloat16)
                     send_low(span + 1, which)
 
-        lax.fori_loop(0, heads, answer, 0)
-        collect()
-        refresh()
+        if span + 1 < spans:
+            collect()
+            refresh()
+        lax.fori_loop(0, heads // 2, answer, 0)
+        if span + 1 == spans:
+            collect()
+            refresh()
         att_ref[span, :, own_columns] = out_buf[span, head]
 
     for span in range(spans):
@@ -479,10 +542,15 @@
                 token_copy(span, kind, other, other, other).wait_send()
         for step in range(1, groups):
             other = within(step)
-            for which in range(3):
-                low_copy(span, which, other, other).wait_send()
-                grad_copy(span, which, other, other).wait_send()
             square_copy(span, other, other).wait_send()
+        for which in range(3):
+            mate_copy(span, which).wait_send()
+            low_copy(span, which, member, mate, 0).wait_send()
+            for step in range(1, pairs_here):
+                other = alike(step)
+                low_copy(span, which, member, other, 0).wait_send()
+                low_copy(span, which, other, mate, 1).wait_send()
+                grad_copy(span, which, pair, lax.div(other, 2)).wait_send()
 
 
 def per_device_fused(
@@ -510,24 +578,28 @@
             pltpu.VMEM((spans, 3, heads, count, width), low),
             pltpu.VMEM((spans, heads, count, width), low),
             pltpu.VMEM((spans, 3, block, width), low),
-            pltpu.VMEM((spans, 3, block, width), low),
+            pltpu.VMEM((spans, 3, 2, groups // 2, rows, width), low),
             pltpu.VMEM((3, block, width), jnp.float32),
-            pltpu.VMEM((spans, 3, groups, rows, width), low),
+            pltpu.VMEM((spans, 3, groups // 2, rows, width), low),
+            pltpu.VMEM((spans, 3, groups // 2, rows, width), low),
+            pltpu.VMEM((spans, 3, groups // 2, rows, width), low),
             pltpu.VMEM((3, rows, width), jnp.float32),
             pltpu.VMEM((3, rows, width), jnp.float32),
-            pltpu.VMEM((heads, count, width), low),
-            pltpu.VMEM((heads, count, width), low),
-            pltpu.VMEM((heads, count, width), low),
+            pltpu.VMEM((heads // 2, 2 * count, width), low),
+            pltpu.VMEM((heads // 2, 2 * count, width), low),
+            pltpu.VMEM((heads // 2, 2 * count, width), low),
             pltpu.VMEM((spans, 3, 8, 128), jnp.float32),
             pltpu.VMEM((spans, groups, 3, 8, 128), jnp.float32),
             dma((spans, 3, heads)),
             dma((spans, 3, heads)),
             dma((spans, heads)),
             dma((spans, heads)),
+            dma((spans, 3, 2, groups)),
             dma((spans, 3, groups)),
-            dma((spans, 3, groups)),
-            dma((spans, 3, groups)),
-            dma((spans, 3, groups)),
+            dma((spans, 3)),
+            dma((spans, 3)),
+            dma((spans, 3, groups // 2)),
+            dma((spans, 3, groups // 2)),
             dma((spans, groups)),
             dma((spans, groups)),
         ],
@@ -554,7 +626,8 @@
         and rows % 16 == 0
         and width % 128 == 0
         and count % 16 == 0
-        and 2 <= groups <= 8
+        and heads % 2 == 0
+        and groups in (2, 4, 6, 8)
     )
     if fits:
         return per_device_fused(heads, groups, *arguments)

time: 86.9 us -> 85.5 us (0.984)
  the two profiles are of different devices: /device:TPU:9 before, /device:TPU:0 now
where the time goes in v3:
time: 85.5 us; the launch traced here: 85.1 us
  Pallas kernels  74.7 us (87%)
  local copies, waits for them, and re-layouts  9.8 us (11%)
    pallas_call x1, Pallas kernels, per_device_fused(): pl.pallas_call(functools.partial(fused_kernel, heads, groups), out_shape=...  74.7 us
    unnamed x17, local copies, waits for them, and re-layouts  9.8 us

profile of v3, /device:TPU:0, one launch (start us, length us, event | category | flops | bytes accessed | tf_op | source)
XLA Modules:
  0.0 85.1 jit_solution(12044346959134718089)
XLA Ops:
  0.6 0.8 copy.11.r_ref
  1.5 0.0 copy-start
  1.5 1.1 %copy-done = bf16[2,128,1536]{2,1,0:T(8,128)(2,1)S(1)} copy-done((bf16[2,128,1536]{2,1,0:T(8,128)(2,1)S(1)}, bf16[2,128,1536]{2,1,0:T(8,128)(2,1)}, u32[]{:S(2)}) %copy-start) | copy-done | bytes 786456
  2.6 0.0 copy-start.1
  2.6 1.1 %copy-done.1 = bf16[2,128,1536]{2,1,0:T(8,128)(2,1)S(1)} copy-done((bf16[2,128,1536]{2,1,0:T(8,128)(2,1)S(1)}, bf16[2,128,1536]{2,1,0:T(8,128)(2,1)}, u32[]{:S(2)}) %copy-start.1) | copy-done | bytes 786456
  3.7 0.0 copy-start.2
  3.7 1.1 %copy-done.2 = bf16[2,128,1536]{2,1,0:T(8,128)(2,1)S(1)} copy-done((bf16[2,128,1536]{2,1,0:T(8,128)(2,1)S(1)}, bf16[2,128,1536]{2,1,0:T(8,128)(2,1)}, u32[]{:S(2)}) %copy-start.2) | copy-done | bytes 786456
  4.9 0.0 copy-start.3
  4.9 0.9 %copy-done.3 = f32[96,384]{1,0:T(8,128)S(1)} copy-done((f32[96,384]{1,0:T(8,128)S(1)}, f32[96,384]{1,0:T(8,128)}, u32[]{:S(2)}) %copy-start.3) | copy-done | bytes 147480
  5.8 0.0 copy-start.4
  5.8 0.9 %copy-done.4 = f32[96,384]{1,0:T(8,128)S(1)} copy-done((f32[96,384]{1,0:T(8,128)S(1)}, f32[96,384]{1,0:T(8,128)}, u32[]{:S(2)}) %copy-start.4) | copy-done | bytes 147480
  6.7 0.0 copy-start.5
  6.7 0.9 %copy-done.5 = f32[96,384]{1,0:T(8,128)S(1)} copy-done((f32[96,384]{1,0:T(8,128)S(1)}, f32[96,384]{1,0:T(8,128)}, u32[]{:S(2)}) %copy-start.5) | copy-done | bytes 147480
  7.6 74.7 %shard_map.102 = (bf16[2,128,1536]{2,1,0:T(8,128)(2,1)S(1)}, f32[96,384]{1,0:T(8,128)S(1)}, f32[96,384]{1,0:T(8,128)S(1)}, f32[96,384]{1,0:T(8,128)S(1)}) custom-call(bf16[2,128,1536]{2,1,0:T(8,128)(2,1)S(1)} %copy-done, bf16[2,128,1536]{2,1,0:T(8,128)(2,1)S(1)} %copy-done.1, bf16[2,128,1536]{2,1,0:T(8,128)(2,1)S(1)} %copy-done.2, ...), custom_call_target="tpu_custom_call" | custom-call | tf_op jit(solution)/shard_map/pallas_call | solution.py:566
  82.3 0.9 %copy.16 = bf16[2,128,1536]{2,1,0:T(8,128)(2,1)} copy(bf16[2,128,1536]{2,1,0:T(8,128)(2,1)S(1)} %get-tuple-element.8) | data formatting | bytes 1572864
  83.2 0.7 copy.17
  83.8 0.7 copy.18
  84.5 0.7 copy.19
Async XLA Ops:
  1.5 1.1 %copy-start = (bf16[2,128,1536]{2,1,0:T(8,128)(2,1)S(1)}, bf16[2,128,1536]{2,1,0:T(8,128)(2,1)}, u32[]{:S(2)}) copy-start(bf16[2,128,1536]{2,1,0:T(8,128)(2,1)} %q_ref.1) | copy-start | bytes 2359300
  2.6 1.1 %copy-start.1 = (bf16[2,128,1536]{2,1,0:T(8,128)(2,1)S(1)}, bf16[2,128,1536]{2,1,0:T(8,128)(2,1)}, u32[]{:S(2)}) copy-start(bf16[2,128,1536]{2,1,0:T(8,128)(2,1)} %k_ref.1) | copy-start | bytes 2359300
  3.7 1.1 %copy-start.2 = (bf16[2,128,1536]{2,1,0:T(8,128)(2,1)S(1)}, bf16[2,128,1536]{2,1,0:T(8,128)(2,1)}, u32[]{:S(2)}) copy-start(bf16[2,128,1536]{2,1,0:T(8,128)(2,1)} %v_ref.1) | copy-start | bytes 2359300
  4.9 0.9 %copy-start.3 = (f32[96,384]{1,0:T(8,128)S(1)}, f32[96,384]{1,0:T(8,128)}, u32[]{:S(2)}) copy-start(f32[96,384]{1,0:T(8,128)} %gate_ref.1) | copy-start | bytes 442372
  5.8 0.9 %copy-start.4 = (f32[96,384]{1,0:T(8,128)S(1)}, f32[96,384]{1,0:T(8,128)}, u32[]{:S(2)}) copy-start(f32[96,384]{1,0:T(8,128)} %up_ref.1) | copy-start | bytes 442372
  6.7 0.9 %copy-start.5 = (f32[96,384]{1,0:T(8,128)S(1)}, f32[96,384]{1,0:T(8,128)}, u32[]{:S(2)}) copy-start(f32[96,384]{1,0:T(8,128)} %down_ref.1) | copy-start | bytes 442372
